TPU v7x, 256 devices: a whole 4x4x8 slice. The times are simulated.
256 devices in a mesh: basis: 16 (over x_hi, z), ex: 16 (over y, x_lo, core).
Axes of the slice: x: 4 (x_hi: 2, x_lo: 2; x = x_hi * 2 + x_lo), y: 4, z: 8, core: 2. Of those that a mesh axis runs over, the one named last changes fastest.
Arguments:
- activations: bfloat16 [2048, 27648], P('ex', 'basis'), may hold values from -6 to 6
- out_grads: bfloat16 [2048, 5120], P('ex'), may hold values from -6 to 6
- act_basis: bfloat16 [27648, 18432], P('basis', 'ex'), may hold values from -0.0390625 to 0.0390625
- grad_basis: bfloat16 [5120, 5120], P(None, 'basis'), may hold values from -0.078125 to 0.078125
- ex_lengths: int32 [16, 5], replicated, may hold values from 1 to 36, 128 in all within a row
Outputs:
- eigenvalues: float32 [5120, 18432], P('basis', 'ex')
Inputs may be any that keep to these rules, and one draw needn't show every extreme that they name: `ex_lengths`: each row sums to 128, and in every row some entry equals 36.
All inputs are finite; a program needn't handle non-finite values.
Results may differ from a plain program's by a relative error of at most 0.0014.
Values may be sent and summed in bfloat16 or wider, within the bound.
No kernel may reach another device: no remote copies, remote signals or barrier semaphores. Data moves between devices by JAX's collectives and lax.ppermute only.
A program may use at most 128 MiB of HBM per device.

v0:
```python
import jax
import jax.numpy as jnp
from jax import lax
from jax.sharding import PartitionSpec as P

MOST = 36


def on_device(activations, out_grads, act_basis, grad_basis, ex_lengths):
    tok_ex = out_grads.shape[0]
    ex_devices = lax.axis_size("ex")
    token_count = tok_ex * ex_devices
    grad_local = jnp.dot(out_grads, grad_basis, preferred_element_type=jnp.float32).astype(
        jnp.bfloat16
    )
    grad_coeffs = lax.all_gather(grad_local, "ex", axis=0, tiled=True)
    act_gathered = lax.all_gather(activations, "ex", axis=0, tiled=True)
    own_share = lax.psum_scatter(
        jnp.dot(act_gathered, act_basis, preferred_element_type=jnp.float32),
        "basis",
        scatter_dimension=0,
        tiled=True,
    )
    act_coeffs = lax.all_gather(own_share.astype(jnp.bfloat16), "basis", axis=0, tiled=True)
    slot_count = MOST
    local_ends = jnp.cumsum(ex_lengths, axis=1)
    local_starts = local_ends - ex_lengths
    act_blocks = act_coeffs.reshape(ex_devices, tok_ex, act_coeffs.shape[1])
    grad_blocks = grad_coeffs.reshape(ex_devices, tok_ex, grad_coeffs.shape[1])
    offsets = jnp.arange(slot_count, dtype=jnp.int32)
    initial = jnp.zeros((grad_coeffs.shape[1], act_coeffs.shape[1]), jnp.float32)

    def block_step(accumulated, block):
        act_block, grad_block, start_row, length_row = block
        slot_index = jnp.minimum(start_row[:, None] + offsets[None, :], tok_ex - 1)
        slot_keep = (offsets[None, :] < length_row[:, None]).astype(jnp.bfloat16)[:, :, None]
        rows_act = act_block[slot_index] * slot_keep
        rows_grad = grad_block[slot_index] * slot_keep
        coeffs = jnp.einsum("esi,esj->eij", rows_grad, rows_act, preferred_element_type=jnp.float32)
        return (accumulated + jnp.sum(coeffs * coeffs, axis=0), None)

    accumulated, _ = lax.scan(
        block_step, initial, (act_blocks, grad_blocks, local_starts, ex_lengths)
    )
    return accumulated / jnp.float32(token_count)


def solution(mesh):
    in_specs = (P("ex", "basis"), P("ex", None), P("basis", "ex"), P(None, "basis"), P())
    out_specs = P("basis", "ex")
    return jax.shard_map(
        on_device, mesh=mesh, in_specs=in_specs, out_specs=out_specs, check_vma=False
    )
```

profile of v0, /device:TPU:8, one launch (start us, length us, event | category | flops | bytes accessed | tf_op | source)
XLA Modules:
  0.0 728.5 jit_solution(14464228511254044016)
XLA Ops:
  7.3 65.5 %all-gather.6.cloned.1.call-done = bf16[2048,1728]{0,1:T(8,128)(2,1)} async-done(((bf16[128,1728]{0,1:T(8,128)(2,1)}), bf16[2048,1728]{0,1:T(8,128)(2,1)}) %all-gather.6.cloned.1.call-update) | async-done | bytes 7077904 | tf_op jit(solution)/shard_map/all_gather | solution.py:17
  72.8 15.4 %fusion.10 = f32[2048,1152]{1,0:T(8,128)} fusion(bf16[2048,1728]{0,1:T(8,128)(2,1)} %all-gather.6.cloned.1.call-done, bf16[1728,1152]{1,0:T(8,128)(2,1)} %param.9), kind=kOutput, calls=%fused_computation.23 | convolution fusion | flops 8153726976 | bytes 20496384 | tf_op jit(solution)/shard_map/dot_general | solution.py:19
  91.3 225.6 %reduce-scatter.2.cloned.1.call-done = f32[128,1152]{1,0:T(8,128)} async-done(((f32[2048,1152]{1,0:T(8,128)}), f32[128,1152]{1,0:T(8,128)}) %reduce-scatter.2.cloned.1.call-update) | async-done | bytes 589840 | tf_op jit(solution)/shard_map/reduce_scatter | solution.py:18
  318.9 34.8 %all-gather.4.cloned.1.call-done = bf16[2048,320]{0,1:T(8,128)(2,1)} async-done(((bf16[128,320]{0,1:T(8,128)(2,1)}), bf16[2048,320]{0,1:T(8,128)(2,1)}) %all-gather.4.cloned.1.call-update) | async-done | bytes 1310736 | tf_op jit(solution)/shard_map/all_gather | solution.py:16
  356.3 104.7 %all-gather.8.cloned.1.call-done = bf16[2048,1152]{1,0:T(8,128)(2,1)} async-done(((bf16[128,1152]{1,0:T(8,128)(2,1)}), bf16[2048,1152]{1,0:T(8,128)(2,1)}) %all-gather.8.cloned.1.call-update) | async-done | bytes 4718608 | tf_op jit(solution)/shard_map/all_gather | solution.py:24
  461.0 258.4 %while.12 = (s32[]{:T(128)}, f32[320,1152]{1,0:T(8,128)}, bf16[16,128,320]{2,1,0:T(8,128)(2,1)}, s32[16,5]{1,0:T(8,128)S(1)}, s32[16,5]{1,0:T(8,128)S(1)}, /*ind...) while((s32[]{:T(128)}, f32[320,1152]{1,0:T(8,128)}, ...), condition=%wide.region_4.5_spmd.clone.clone, body=%wide.region_2.4_spmd.clone.clone.sunk | while | flops 137032688 | bytes 9310867 | solution.py:42
  470.5 3.6 multiply_reduce_fusion.2
  486.2 3.6 multiply_reduce_fusion.2
  502.4 3.6 multiply_reduce_fusion.2
  518.6 3.6 multiply_reduce_fusion.2
  534.7 3.6 multiply_reduce_fusion.2
  543.3 3.1 gather_fusion
  550.9 3.6 multiply_reduce_fusion.2
  559.5 3.1 gather_fusion
  567.1 3.6 multiply_reduce_fusion.2
  583.3 3.6 multiply_reduce_fusion.2
  599.5 3.6 multiply_reduce_fusion.2
  615.6 3.6 multiply_reduce_fusion.2
  631.8 3.6 multiply_reduce_fusion.2
  648.0 3.6 multiply_reduce_fusion.2
  664.2 3.6 multiply_reduce_fusion.2
  680.3 3.6 multiply_reduce_fusion.2
  696.5 3.6 multiply_reduce_fusion.2
  712.7 3.6 multiply_reduce_fusion.2
  (210 shorter events, 205.7 us)
Async XLA Ops:
  6.5 81.7 %copy-start = (bf16[5120,320]{0,1:T(8,128)(2,1)S(1)}, bf16[5120,320]{0,1:T(8,128)(2,1)}, u32[]{:S(2)}) copy-start(bf16[5120,320]{0,1:T(8,128)(2,1)} %param.10) | copy-start | bytes 9830404
  6.5 66.2 %all-gather.6.cloned.1.call-start = ((), (), s32[]{:S(2)}) async-start(), calls=%async_computation.2 | async-start | bytes 7520256 | tf_op jit(solution)/shard_map/all_gather | solution.py:17
  7.3 309.6 %reduce-scatter.2.cloned.1.call-start = ((), (), s32[]{:S(2)}) async-start(), calls=%async_computation.3 | async-start | bytes 10027008 | tf_op jit(solution)/shard_map/reduce_scatter | solution.py:18
  88.2 230.5 %copy-start.1 = (s32[16,5]{0,1:T(8,128)S(1)}, s32[16,5]{0,1:T(8,128)}, u32[]{:S(2)}) copy-start(s32[16,5]{0,1:T(8,128)} %param.11) | copy-start | bytes 964
  88.2 265.5 %all-gather.4.cloned.1.call-start = ((), (), s32[]{:S(2)}) async-start(), calls=%async_computation.1 | async-start | bytes 1392640 | tf_op jit(solution)/shard_map/all_gather | solution.py:16
  91.2 369.7 %all-gather.8.cloned.1.call-start = ((), (), s32[]{:S(2)}) async-start(), calls=%async_computation.4 | async-start | bytes 5013504 | tf_op jit(solution)/shard_map/all_gather | solution.py:24
Sparse Core Ops, SparseCore 0:
  9.1 63.5 all-gather.5
  88.3 228.4 reduce-scatter.1
  318.7 34.9 all-gather.3
  356.5 104.4 all-gather.7
where the time goes:
time: 732 us; the launch traced here: 728 us
  waiting for transfers between devices  431 us (59%)
  local copies, waits for them, and re-layouts  152 us (21%)
  matrix products  75.7 us (10%)
  other arithmetic  55.8 us (8%)
  between operations  13.2 us (2%)
    reduce_scatter x1, waiting for transfers between devices, on_device(): lax.psum_scatter(jnp.dot(act_gathered, act_basis, preferred_element_type=...  226 us
    all_gather x1, waiting for transfers between devices, on_device(): lax.all_gather(own_share.astype(jnp.bfloat16), 'basis', axis=0, tiled=True)  105 us
    gather x32, local copies, waits for them, and re-layouts, block_step(): rows_act = act_block[slot_index] * slot_keep  79.3 us
    all_gather x1, waiting for transfers between devices, on_device(): act_gathered = lax.all_gather(activations, 'ex', axis=0, tiled=True)  65.5 us
    dot_general x16, matrix products, block_step(): jnp.einsum('esi,esj->eij', rows_grad, rows_act, preferred_element_type=jn...  57.4 us
    add x16, other arithmetic, block_step(): return (accumulated + jnp.sum(coeffs * coeffs, axis=0), None)  48.8 us
    squeeze x32, local copies, waits for them, and re-layouts, on_device(): lax.scan(block_step, initial, (act_blocks, grad_blocks, local_starts, ex_...  41.7 us
    all_gather x1, waiting for transfers between devices, on_device(): grad_coeffs = lax.all_gather(grad_local, 'ex', axis=0, tiled=True)  34.8 us
  transfers between devices with their start and end apart: 4, of which 4 were waited for; matrix products, arithmetic and copies ran while one was open for 1% of the time, Pallas kernels for 0%

commit v1 on v0

v1 whole, which is shorter than its diff:
```python
import jax
import jax.numpy as jnp
from jax import lax
from jax.experimental import pallas as pl
from jax.experimental.pallas import tpu as pltpu
from jax.sharding import PartitionSpec as P

Z, X_HI = 8, 2
Y, X_LO, CORE = 4, 2, 2
BLOCK = 128
EXB = 5
WIDE = 256


def shift_z(value, by):
    pairs = [(x * Z + z, x * Z + (z + by) % Z) for x in range(X_HI) for z in range(Z)]
    return lax.ppermute(value, "basis", pairs)


def swap_x(value):
    pairs = [(x * Z + z, (1 - x) * Z + z) for x in range(X_HI) for z in range(Z)]
    return lax.ppermute(value, "basis", pairs)


def ex_index(y, x, c):
    return (y * X_LO + x) * CORE + c


def shift_ex(value, dy, dx, dc):
    pairs = [
        (ex_index(y, x, c), ex_index((y + dy) % Y, (x + dx) % X_LO, (c + dc) % CORE))
        for y in range(Y)
        for x in range(X_LO)
        for c in range(CORE)
    ]
    return lax.ppermute(value, "ex", pairs)


def both_cores(parts):
    mine = jnp.concatenate(parts, axis=0) if len(parts) > 1 else parts[0]
    return [mine, shift_ex(mine, 0, 0, 1)]


def gather_groups(own):
    rows = own.shape[0]
    up, down, side = (0, 1), (0, -1), (1, 0)
    first_y = shift_ex(own, 1, 0, 0)
    second_y = shift_ex(own, -1, 0, 0)
    beside = shift_ex(own, 0, 1, 0)
    far = shift_ex(first_y, 1, 0, 0)
    beside_up = shift_ex(beside, -1, 0, 0)
    beside_down = shift_ex(first_y, 0, 1, 0)
    a, b = 48, 96
    last = [
        shift_ex(beside_down[:a], 1, 0, 0),
        shift_ex(beside_up[a:b], -1, 0, 0),
        shift_ex(far[b:], 0, 1, 0),
    ]
    groups = [[own], [first_y, second_y, beside], [far, beside_up, beside_down], [jnp.concatenate(last, 0)]]
    places = [[(0, 0)], [(-1, 0), (1, 0), (0, 1)], [(2, 0), (1, 1), (-1, 1)], [(2, 1)]]
    arrays, order = [], []
    for parts, place in zip(groups, places):
        arrays.append(both_cores(parts))
        order.append([(dy, dx, dc) for dc in range(CORE) for dy, dx in place])
    return arrays, order


def sum_over_basis(partial_of, chunk):
    bf = jnp.bfloat16
    half = chunk // 2
    farthest = partial_of(4).astype(bf)
    going_down = shift_z(farthest[:half], -1)
    going_up = shift_z(farthest[half:], 1)
    for k in (3, 2, 1):
        low, high = partial_of(-k), partial_of(k)
        if k == 3:
            low = jnp.concatenate([low[:half] + going_down, low[half:]], 0)
            high = jnp.concatenate([high[:half], high[half:] + going_up], 0)
        else:
            low, high = low + going_down, high + going_up
        going_down = shift_z(low.astype(bf), -1)
        going_up = shift_z(high.astype(bf), 1)
    total = partial_of(0) + going_down + going_up
    return (total + swap_x(total.astype(bf))).astype(bf)


def gather_over_z(value):
    groups = [[x * Z + z for z in range(Z)] for x in range(X_HI)]
    return lax.all_gather(value, "basis", axis=0, tiled=True, axis_index_groups=groups)


def outer_kernel(scale, at_ref, bounds_ref, grad_ref, act_ref, out_ref):
    blocks, high, block = grad_ref.shape
    wide = act_ref.shape[1]
    token = lax.broadcasted_iota(jnp.int32, (high, block), 1)
    out_ref[...] = jnp.zeros_like(out_ref)

    def step(b, carry):
        at = at_ref[b]
        grads = grad_ref[at]
        zeros = jnp.zeros_like(grads)
        rows = pl.ds(pl.multiple_of(b * block, block), block)
        lhs = jnp.concatenate(
            [
                jnp.where((token >= bounds_ref[at, e]) & (token < bounds_ref[at, e + 1]), grads, zeros)
                for e in range(EXB)
            ],
            axis=0,
        )
        for n in range(0, wide, WIDE):
            columns = slice(n, min(n + WIDE, wide))
            coeffs = jnp.dot(lhs, act_ref[rows, columns], preferred_element_type=jnp.float32)
            squares = coeffs * coeffs
            total = squares[:high]
            for e in range(1, EXB):
                total = total + squares[e * high : (e + 1) * high]
            out_ref[:, columns] += total
        return carry

    lax.fori_loop(0, blocks, step, 0, unroll=2)
    out_ref[...] = out_ref[...] * scale


def squared_sums(at, bounds, grads, acts, token_count):
    vmem = pl.BlockSpec(memory_space=pltpu.VMEM)
    smem = pl.BlockSpec(memory_space=pltpu.SMEM)
    blocks, high, block = grads.shape
    return pl.pallas_call(
        lambda *refs: outer_kernel(1.0 / token_count, *refs),
        out_shape=jax.ShapeDtypeStruct((high, acts.shape[1]), jnp.float32),
        in_specs=[smem, smem, vmem, vmem],
        out_specs=vmem,
        compiler_params=pltpu.CompilerParams(vmem_limit_bytes=40 * 1024 * 1024),
        cost_estimate=pl.CostEstimate(
            flops=2 * EXB * acts.size * high, bytes_accessed=2 * acts.size, transcendentals=0
        ),
    )(at, bounds, grads, acts)


def on_device(activations, out_grads, act_basis, grad_basis, ex_lengths):
    token_count = out_grads.shape[0] * lax.axis_size("ex")
    z = lax.axis_index("basis") % Z
    ex = lax.axis_index("ex")
    y, x, c = ex // (X_LO * CORE), (ex // CORE) % X_LO, ex % CORE

    grad_local = lax.dot_general(
        grad_basis, out_grads, (((0,), (1,)), ((), ())), preferred_element_type=jnp.float32
    ).astype(jnp.bfloat16)
    grads = lax.all_gather(grad_local, "ex", axis=0)

    arrays, order = gather_groups(activations)
    arrays[-1], grads = lax.optimization_barrier((arrays[-1], grads))
    streams = STREAMS
    acts, places = [], []
    for stream in streams:
        tokens = jnp.concatenate([a for g in stream for a in arrays[g]], axis=0)
        for g in stream:
            places += order[g]
        chunk = tokens.shape[0] // Z

        def partial_of(k, tokens=tokens, chunk=chunk):
            rows = lax.dynamic_slice_in_dim(tokens, ((z + k) % Z) * chunk, chunk, 0)
            return jnp.dot(rows, act_basis, preferred_element_type=jnp.float32)

        acts.append(gather_over_z(sum_over_basis(partial_of, chunk)))

    at = jnp.stack(
        [((y + dy) % Y * X_LO + (x + dx) % X_LO) * CORE + (c + dc) % CORE for dy, dx, dc in places]
    ).astype(jnp.int32)
    ends = jnp.cumsum(ex_lengths, axis=1)
    bounds = jnp.concatenate([jnp.zeros_like(ends[:, :1]), ends], axis=1).astype(jnp.int32)
    act_coeffs = jnp.concatenate(acts, axis=0) if len(acts) > 1 else acts[0]
    return squared_sums(at, bounds, grads, act_coeffs, token_count)


STREAMS = ((0, 1, 2, 3),)


def solution(mesh):
    in_specs = (P("ex", "basis"), P("ex", None), P("basis", "ex"), P(None, "basis"), P())
    out_specs = P("basis", "ex")
    return jax.shard_map(
        on_device, mesh=mesh, in_specs=in_specs, out_specs=out_specs, check_vma=False
    )
```

time: 732 us -> 257 us (0.35)
  waiting for transfers between devices: 431 us -> 137 us
  local copies, waits for them, and re-layouts: 152 us -> 18.2 us
  other arithmetic: 55.8 us -> 5 us
  matrix products: 75.7 us -> 32.7 us
  starting transfers between devices: 0.12 us -> 30.5 us
  Pallas kernels: 0 us -> 18.5 us
    reduce_scatter x1 -> x0, waiting for transfers between devices: 226 us -> none  [on_device(): lax.psum_scatter(jnp.dot(act_gathered, act_basis, preferred_element_type=...]
    all_gather x3 -> x2, waiting for transfers between devices: 205 us -> 59 us  [the longest x1 59 us: gather_over_z(): lax.all_gather(value, 'basis', axis=0, tiled=True, axis_index_groups=groups)]
    gather x64 -> x0, local copies, waits for them, and re-layouts: 106 us -> none  [the longest x32 79.3 us: block_step(): rows_act = act_block[slot_index] * slot_keep]
    ppermute x0 -> x22, waiting for transfers between devices: none -> 78.1 us  [the longest x8 38.7 us: shift_z(): return lax.ppermute(value, 'basis', pairs)]
    add x16 -> x0, other arithmetic: 48.8 us -> none  [block_step(): return (accumulated + jnp.sum(coeffs * coeffs, axis=0), None)]
    dot_general x18 -> x9, matrix products: 75.7 us -> 32.7 us  [the longest x8 29.7 us: partial_of(): return jnp.dot(rows, act_basis, preferred_element_type=jnp.float32)]
    squeeze x32 -> x0, local copies, waits for them, and re-layouts: 41.7 us -> none  [on_device(): lax.scan(block_step, initial, (act_blocks, grad_blocks, local_starts, ex_...]
    ppermute x0 -> x22, starting transfers between devices: none -> 30.4 us  [the longest x8 15.9 us: shift_z(): return lax.ppermute(value, 'basis', pairs)]
  transfers between devices with their start and end apart: 4 -> 24, of which waited for: 4 -> 15; matrix products, arithmetic and copies ran while one was open for 1% -> 13% of each run, Pallas kernels for 0% -> 0%
where the time goes in v1:
time: 257 us; the launch traced here: 256 us
  waiting for transfers between devices  137 us (53%)
  matrix products  32.7 us (13%)
  starting transfers between devices  30.5 us (12%)
  Pallas kernels  18.5 us (7%)
  local copies, waits for them, and re-layouts  18.2 us (7%)
  between operations  13.9 us (5%)
  other arithmetic  5 us (2%)
    all_gather x1, waiting for transfers between devices, gather_over_z(): lax.all_gather(value, 'basis', axis=0, tiled=True, axis_index_groups=groups)  59 us
    ppermute x8, waiting for transfers between devices, shift_z(): return lax.ppermute(value, 'basis', pairs)  38.7 us
    dot_general x8, matrix products, partial_of(): return jnp.dot(rows, act_basis, preferred_element_type=jnp.float32)  29.7 us
    ppermute x13, waiting for transfers between devices, shift_ex(): return lax.ppermute(value, 'ex', pairs)  28.9 us
    pallas_call x1, Pallas kernels, squared_sums(): pl.pallas_call(lambda *refs: outer_kernel(1.0 / token_count, *refs), out_...  18.5 us
    ppermute x8, starting transfers between devices, shift_z(): return lax.ppermute(value, 'basis', pairs)  15.9 us
    unnamed x30, local copies, waits for them, and re-layouts  15.5 us
    ppermute x13, starting transfers between devices, shift_ex(): return lax.ppermute(value, 'ex', pairs)  11.5 us
  transfers between devices with their start and end apart: 24, of which 15 were waited for; matrix products, arithmetic and copies ran while one was open for 13% of the time, Pallas kernels for 0%

profile of v1, /device:TPU:8, one launch (start us, length us, event | category | flops | bytes accessed | tf_op | source)
XLA Modules:
  0.0 255.9 jit_solution(7678771503850982111)
XLA Ops:
  10.1 3.0 %convolution_convert_fusion.1 = bf16[320,128]{1,0:T(8,128)(2,1)} fusion(bf16[5120,320]{0,1:T(8,128)(2,1)S(1)} %copy-done, bf16[128,5120]{1,0:T(8,128)(2,1)} %param.6), kind=kOutput, calls=%fused_computation.14 | convolution fusion | flops 419471360 | bytes 4669440 | tf_op jit(solution)/shard_map/dot_general | solution.py:146
  14.3 4.4 %collective-permute-done = bf16[128,1728]{0,1:T(8,128)(2,1)} collective-permute-done((bf16[128,1728]{0,1:T(8,128)(2,1)}, bf16[128,1728]{0,1:T(8,128)(2,1)}, u32[]{:S(2)}, u32[]{:S(2)}) %collective-permute-start) | collective-permute-done | bytes 442400 | tf_op jit(solution)/shard_map/ppermute | solution.py:36
  30.1 10.3 %collective-permute-done.6 = bf16[128,1728]{0,1:T(8,128)(2,1)S(1)} collective-permute-done((bf16[128,1728]{0,1:T(8,128)(2,1)}, bf16[128,1728]{0,1:T(8,128)(2,1)S(1)}, u32[]{:S(2)}, u32[]{:S(2)}) %collective-permute-start.6) | collective-permute-done | bytes 442400 | tf_op jit(solution)/shard_map/ppermute | solution.py:36
  47.2 7.5 %collective-permute-done.7 = bf16[32,1728]{0,1:T(8,128)(2,1)S(1)} collective-permute-done((bf16[32,1728]{0,1:T(8,128)(2,1)S(1)}, bf16[32,1728]{0,1:T(8,128)(2,1)S(1)}, u32[]{:S(2)}, u32[]{:S(2)}) %collective-permute-start.7) | collective-permute-done | bytes 110624 | tf_op jit(solution)/shard_map/ppermute | solution.py:36
  59.6 2.9 %copy-done.4 = bf16[2048,1728]{0,1:T(8,128)(2,1)} copy-done((bf16[2048,1728]{0,1:T(8,128)(2,1)}, bf16[2048,1728]{0,1:T(8,128)(2,1)S(1)}, u32[]{:S(2)}) %copy-start.4) | copy-done | bytes 7077912
  66.4 3.8 %fusion.10 = f32[256,1152]{1,0:T(8,128)S(1)} fusion(bf16[1728,1152]{1,0:T(8,128)(2,1)} %param.7, bf16[2048,1728]{0,1:T(8,128)(2,1)} %constant_dynamic-update-slice_fusion, s32[]{:T(128)S(6)} %select_n.210), kind=kOutput, calls=%fused_computation.20 | convolution fusion | flops 1019215872 | bytes 6045700 | tf_op jit(solution)/shard_map/dot_general | solution.py:163
  72.9 4.8 %collective-permute-start.13 = (bf16[128,1152]{1,0:T(8,128)(2,1)S(1)}, bf16[128,1152]{1,0:T(8,128)(2,1)S(1)}, u32[]{:S(2)}, u32[]{:S(2)}) collective-permute-start(bf16[128,1152]{1,0:T(8,128)(2,1)S(1)} %get-tuple-element.11), channel_id=1, source_target_pairs={{0,112},{16,0},{32,16},{48,32},{64,48},{80,64},{96,80},{112,96},{1... | collective-permute-start | bytes 884744 | tf_op jit(solution)/shard_map/ppermute | solution.py:17
  80.4 4.2 %collective-permute-done.13 = bf16[128,1152]{1,0:T(8,128)(2,1)S(1)} collective-permute-done((bf16[128,1152]{1,0:T(8,128)(2,1)S(1)}, bf16[128,1152]{1,0:T(8,128)(2,1)S(1)}, u32[]{:S(2)}, u32[]{:S(2)}) %collective-permute-start.13) | collective-permute-done | bytes 294944 | tf_op jit(solution)/shard_map/ppermute | solution.py:17
  85.5 3.7 %collective-permute-start.14 = (bf16[256,1152]{1,0:T(8,128)(2,1)}, bf16[256,1152]{1,0:T(8,128)(2,1)}, u32[]{:S(2)}, u32[]{:S(2)}) collective-permute-start(bf16[256,1152]{1,0:T(8,128)(2,1)} %pad_maximum_fusion.2), channel_id=1, source_target_pairs={{0,112},{16,0},{32,16},{48,32},{64,48},{80,64},{96,80},{112,96},{1... | collective-permute-start | bytes 1769480 | tf_op jit(solution)/shard_map/ppermute | solution.py:17
  90.1 11.8 %collective-permute-done.14 = bf16[256,1152]{1,0:T(8,128)(2,1)} collective-permute-done((bf16[256,1152]{1,0:T(8,128)(2,1)}, bf16[256,1152]{1,0:T(8,128)(2,1)}, u32[]{:S(2)}, u32[]{:S(2)}) %collective-permute-start.14) | collective-permute-done | bytes 589856 | tf_op jit(solution)/shard_map/ppermute | solution.py:17
  101.9 4.8 %fusion.2 = bf16[256,1152]{1,0:T(8,128)(2,1)} fusion(bf16[1728,1152]{1,0:T(8,128)(2,1)} %param.7, bf16[256,1152]{1,0:T(8,128)(2,1)} %collective-permute-done.14, bf16[2048,1728]{0,1:T(8,128)(2,1)} %constant_dynamic-update-slice_fusion, s32[]{:T(128)S(6)} %select_n.208), kind=kOutput, calls=%fused_computation.8 | convolution fusion | flops 1020100608 | bytes 6045700 | tf_op jit(solution)/shard_map/dot_general | solution.py:163
  106.7 3.7 %collective-permute-start.15 = (bf16[256,1152]{1,0:T(8,128)(2,1)}, bf16[256,1152]{1,0:T(8,128)(2,1)}, u32[]{:S(2)}, u32[]{:S(2)}) collective-permute-start(bf16[256,1152]{1,0:T(8,128)(2,1)} %fusion.2), channel_id=1, source_target_pairs={{0,112},{16,0},{32,16},{48,32},{64,48},{80,64},{96,80},{112,96},{1... | collective-permute-start | bytes 1769480 | tf_op jit(solution)/shard_map/ppermute | solution.py:17
  110.4 3.6 %fusion.4 = bf16[256,1152]{1,0:T(8,128)(2,1)} fusion(bf16[1728,1152]{1,0:T(8,128)(2,1)S(1)} %copy-done.7, bf16[256,1152]{1,0:T(8,128)(2,1)} %collective-permute-done.18, bf16[2048,1728]{0,1:T(8,128)(2,1)} %constant_dynamic-update-slice_fusion, s32[]{:T(128)S(6)} %select_n.216), kind=kOutput, calls=%fused_computation.10 | convolution fusion | flops 1020100608 | bytes 6045700 | tf_op jit(solution)/shard_map/dot_general | solution.py:163
  114.0 8.3 %collective-permute-done.15 = bf16[256,1152]{1,0:T(8,128)(2,1)} collective-permute-done((bf16[256,1152]{1,0:T(8,128)(2,1)}, bf16[256,1152]{1,0:T(8,128)(2,1)}, u32[]{:S(2)}, u32[]{:S(2)}) %collective-permute-start.15) | collective-permute-done | bytes 589856 | tf_op jit(solution)/shard_map/ppermute | solution.py:17
  122.3 4.8 %fusion.1 = bf16[256,1152]{1,0:T(8,128)(2,1)} fusion(bf16[1728,1152]{1,0:T(8,128)(2,1)} %param.7, bf16[256,1152]{1,0:T(8,128)(2,1)} %collective-permute-done.15, bf16[2048,1728]{0,1:T(8,128)(2,1)} %constant_dynamic-update-slice_fusion, s32[]{:T(128)S(6)} %select_n.206), kind=kOutput, calls=%fused_computation.7 | convolution fusion | flops 1020100608 | bytes 6045700 | tf_op jit(solution)/shard_map/dot_general | solution.py:163
  127.0 3.7 %collective-permute-start.16 = (bf16[256,1152]{1,0:T(8,128)(2,1)}, bf16[256,1152]{1,0:T(8,128)(2,1)}, u32[]{:S(2)}, u32[]{:S(2)}) collective-permute-start(bf16[256,1152]{1,0:T(8,128)(2,1)} %fusion.1), channel_id=1, source_target_pairs={{0,112},{16,0},{32,16},{48,32},{64,48},{80,64},{96,80},{112,96},{1... | collective-permute-start | bytes 1769480 | tf_op jit(solution)/shard_map/ppermute | solution.py:17
  130.7 3.6 %fusion.3 = bf16[256,1152]{1,0:T(8,128)(2,1)} fusion(bf16[1728,1152]{1,0:T(8,128)(2,1)S(1)} %copy-done.8, bf16[256,1152]{1,0:T(8,128)(2,1)} %collective-permute-done.19, bf16[2048,1728]{0,1:T(8,128)(2,1)} %constant_dynamic-update-slice_fusion, s32[]{:T(128)S(6)} %select_n.214), kind=kOutput, calls=%fused_computation.9 | convolution fusion | flops 1020100608 | bytes 6045700 | tf_op jit(solution)/shard_map/dot_general | solution.py:163
  134.3 7.4 %collective-permute-done.16 = bf16[256,1152]{1,0:T(8,128)(2,1)} collective-permute-done((bf16[256,1152]{1,0:T(8,128)(2,1)}, bf16[256,1152]{1,0:T(8,128)(2,1)}, u32[]{:S(2)}, u32[]{:S(2)}) %collective-permute-start.16) | collective-permute-done | bytes 589856 | tf_op jit(solution)/shard_map/ppermute | solution.py:17
  141.7 7.0 %collective-permute-done.20 = bf16[256,1152]{1,0:T(8,128)(2,1)} collective-permute-done((bf16[256,1152]{1,0:T(8,128)(2,1)}, bf16[256,1152]{1,0:T(8,128)(2,1)}, u32[]{:S(2)}, u32[]{:S(2)}) %collective-permute-start.20) | collective-permute-done | bytes 589856 | tf_op jit(solution)/shard_map/ppermute | solution.py:17
  148.7 4.1 %fusion.26 = (bf16[256,1152]{1,0:T(8,128)(2,1)S(1)}, f32[256,1152]{1,0:T(8,128)S(1)}) fusion(bf16[256,1152]{1,0:T(8,128)(2,1)} %collective-permute-done.20, bf16[256,1152]{1,0:T(8,128)(2,1)} %collective-permute-done.16, bf16[1728,1152]{1,0:T(8,128)(2,1)} %param.7, bf16[2048,1728]{0,1:T(8,128)(2,1)} %constant_dynamic-update-slice_fusion, s32[]{:T(128)S(6)} %select_n.204), kind=kOutput, calls=%fused_computation.55 | convolution fusion | flops 1020690432 | bytes 7815172 | tf_op jit(solution)/shard_map/dot_general | solution.py:163
  152.8 3.0 %collective-permute-start.21 = (bf16[256,1152]{1,0:T(8,128)(2,1)S(1)}, bf16[256,1152]{1,0:T(8,128)(2,1)S(1)}, u32[]{:S(2)}, u32[]{:S(2)}) collective-permute-start(bf16[256,1152]{1,0:T(8,128)(2,1)S(1)} %get-tuple-element.13), channel_id=1, source_target_pairs={{0,128},{16,144},{32,160},{48,176},{64,192},{80,208},{96,224},{112... | collective-permute-start | bytes 1769480 | tf_op jit(solution)/shard_map/ppermute | solution.py:22
  155.8 10.5 %collective-permute-done.21 = bf16[256,1152]{1,0:T(8,128)(2,1)S(1)} collective-permute-done((bf16[256,1152]{1,0:T(8,128)(2,1)S(1)}, bf16[256,1152]{1,0:T(8,128)(2,1)S(1)}, u32[]{:S(2)}, u32[]{:S(2)}) %collective-permute-start.21) | collective-permute-done | bytes 589856 | tf_op jit(solution)/shard_map/ppermute | solution.py:22
  167.9 59.0 %all-gather.4.cloned.1.call-done.refs_3_ = bf16[2048,1152]{1,0:T(8,128)(2,1)} async-done(((bf16[256,1152]{1,0:T(8,128)(2,1)}), bf16[2048,1152]{1,0:T(8,128)(2,1)}) %all-gather.4.cloned.1.call-update) | async-done | bytes 4718608 | tf_op jit(solution)/shard_map/all_gather | solution.py:89
  230.6 18.5 %shard_map.55 = f32[320,1152]{1,0:T(8,128)} custom-call(s32[16]{0:T(128)S(1)} %stack.67.refs_0_, s32[16,6]{1,0:T(8,128)S(1)} %concatenate.24.refs_1_, bf16[16,320,128]{2,1,0:T(8,128)(2,1)S(1)} %bitcast.28, bf16[2048,1152]{1,0:T(8,128)(2,1)S(1)} %copy-done.1), custom_call_target="tpu_custom_call" | custom-call | flops 7549747200 | bytes 4718592 | tf_op jit(solution)/shard_map/pallas_call | solution.py:128
  (83 shorter events, 43.8 us)
Async XLA Ops:
  6.5 55.9 %all-gather.6.cloned.1.call-start = ((), (), s32[]{:S(2)}) async-start(), calls=%async_computation.1 | async-start | bytes 1392640 | tf_op jit(solution)/shard_map/all_gather | solution.py:149
  6.5 12.2 %collective-permute-start = (bf16[128,1728]{0,1:T(8,128)(2,1)}, bf16[128,1728]{0,1:T(8,128)(2,1)}, u32[]{:S(2)}, u32[]{:S(2)}) collective-permute-start(bf16[128,1728]{0,1:T(8,128)(2,1)} %param.5), channel_id=1, source_target_pairs={{0,4},{1,5},{2,6},{3,7},{4,8},{5,9},{6,10},{7,11},{8,12},{9,13},{1... | collective-permute-start | bytes 1327112 | tf_op jit(solution)/shard_map/ppermute | solution.py:36
  8.1 18.5 %collective-permute-start.9 = (bf16[128,1728]{0,1:T(8,128)(2,1)}, bf16[128,1728]{0,1:T(8,128)(2,1)}, u32[]{:S(2)}, u32[]{:S(2)}) collective-permute-start(bf16[128,1728]{0,1:T(8,128)(2,1)} %param.5), channel_id=1, source_target_pairs={{0,1},{1,0},{2,3},{3,2},{4,5},{5,4},{6,7},{7,6},{8,9},{9,8},{10,11... | collective-permute-start | bytes 1327112 | tf_op jit(solution)/shard_map/ppermute | solution.py:36
  8.1 12.9 %collective-permute-start.10 = (bf16[128,1728]{0,1:T(8,128)(2,1)}, bf16[128,1728]{0,1:T(8,128)(2,1)}, u32[]{:S(2)}, u32[]{:S(2)}) collective-permute-start(bf16[128,1728]{0,1:T(8,128)(2,1)} %param.5), channel_id=1, source_target_pairs={{0,12},{1,13},{2,14},{3,15},{4,0},{5,1},{6,2},{7,3},{8,4},{9,5},{1... | collective-permute-start | bytes 1327112 | tf_op jit(solution)/shard_map/ppermute | solution.py:36
  8.8 12.5 %collective-permute-start.3 = (bf16[128,1728]{0,1:T(8,128)(2,1)}, bf16[128,1728]{0,1:T(8,128)(2,1)}, u32[]{:S(2)}, u32[]{:S(2)}) collective-permute-start(bf16[128,1728]{0,1:T(8,128)(2,1)} %param.5), channel_id=1, source_target_pairs={{0,2},{1,3},{2,0},{3,1},{4,6},{5,7},{6,4},{7,5},{8,10},{9,11},{10,... | collective-permute-start | bytes 1327112 | tf_op jit(solution)/shard_map/ppermute | solution.py:36
  13.1 213.9 %all-gather.4.cloned.1.call-start = ((), (), s32[]{:S(2)}) async-start(), calls=%async_computation | async-start | bytes 5308416 | tf_op jit(solution)/shard_map/all_gather | solution.py:89
  22.8 35.5 %collective-permute-start.11 = (bf16[384,1728]{0,1:T(8,128)(2,1)S(1)}, bf16[384,1728]{0,1:T(8,128)(2,1)S(1)}, u32[]{:S(2)}, u32[]{:S(2)}) collective-permute-start(bf16[384,1728]{0,1:T(8,128)(2,1)S(1)} %pad_maximum_fusion), channel_id=1, source_target_pairs={{0,1},{1,0},{2,3},{3,2},{4,5},{5,4},{6,7},{7,6},{8,9},{9,8},{10,11... | collective-permute-start | bytes 3981320 | tf_op jit(solution)/shard_map/ppermute | solution.py:36
  22.9 17.5 %collective-permute-start.6 = (bf16[128,1728]{0,1:T(8,128)(2,1)}, bf16[128,1728]{0,1:T(8,128)(2,1)S(1)}, u32[]{:S(2)}, u32[]{:S(2)}) collective-permute-start(bf16[128,1728]{0,1:T(8,128)(2,1)} %collective-permute-done), channel_id=1, source_target_pairs={{0,4},{1,5},{2,6},{3,7},{4,8},{5,9},{6,10},{7,11},{8,12},{9,13},{1... | collective-permute-start | bytes 1327112 | tf_op jit(solution)/shard_map/ppermute | solution.py:36
  24.4 17.1 %collective-permute-start.4 = (bf16[128,1728]{0,1:T(8,128)(2,1)}, bf16[128,1728]{0,1:T(8,128)(2,1)S(1)}, u32[]{:S(2)}, u32[]{:S(2)}) collective-permute-start(bf16[128,1728]{0,1:T(8,128)(2,1)} %collective-permute-done.3), channel_id=1, source_target_pairs={{0,12},{1,13},{2,14},{3,15},{4,0},{5,1},{6,2},{7,3},{8,4},{9,5},{1... | collective-permute-start | bytes 1327112 | tf_op jit(solution)/shard_map/ppermute | solution.py:36
  26.3 15.2 %collective-permute-start.1 = (bf16[128,1728]{0,1:T(8,128)(2,1)}, bf16[128,1728]{0,1:T(8,128)(2,1)S(1)}, u32[]{:S(2)}, u32[]{:S(2)}) collective-permute-start(bf16[128,1728]{0,1:T(8,128)(2,1)} %collective-permute-done), channel_id=1, source_target_pairs={{0,2},{1,3},{2,0},{3,1},{4,6},{5,7},{6,4},{7,5},{8,10},{9,11},{10,... | collective-permute-start | bytes 1327112 | tf_op jit(solution)/shard_map/ppermute | solution.py:36
  41.7 17.5 %collective-permute-start.12 = (bf16[384,1728]{0,1:T(8,128)(2,1)S(1)}, bf16[384,1728]{0,1:T(8,128)(2,1)S(1)}, u32[]{:S(2)}, u32[]{:S(2)}) collective-permute-start(bf16[384,1728]{0,1:T(8,128)(2,1)S(1)} %pad_maximum_fusion.1), channel_id=1, source_target_pairs={{0,1},{1,0},{2,3},{3,2},{4,5},{5,4},{6,7},{7,6},{8,9},{9,8},{10,11... | collective-permute-start | bytes 3981320 | tf_op jit(solution)/shard_map/ppermute | solution.py:36
  42.0 12.7 %collective-permute-start.7 = (bf16[32,1728]{0,1:T(8,128)(2,1)S(1)}, bf16[32,1728]{0,1:T(8,128)(2,1)S(1)}, u32[]{:S(2)}, u32[]{:S(2)}) collective-permute-start(bf16[32,1728]{0,1:T(8,128)(2,1)S(1)} %slice.40), channel_id=1, source_target_pairs={{0,2},{1,3},{2,0},{3,1},{4,6},{5,7},{6,4},{7,5},{8,10},{9,11},{10,... | collective-permute-start | bytes 331784 | tf_op jit(solution)/shard_map/ppermute | solution.py:36
  42.2 15.2 %collective-permute-start.2 = (bf16[48,1728]{0,1:T(8,128)(2,1)S(1)}, bf16[48,1728]{0,1:T(8,128)(2,1)S(1)}, u32[]{:S(2)}, u32[]{:S(2)}) collective-permute-start(bf16[48,1728]{0,1:T(8,128)(2,1)S(1)} %bitcast.29), channel_id=1, source_target_pairs={{0,4},{1,5},{2,6},{3,7},{4,8},{5,9},{6,10},{7,11},{8,12},{9,13},{1... | collective-permute-start | bytes 497672 | tf_op jit(solution)/shard_map/ppermute | solution.py:36
  44.4 13.2 %collective-permute-start.5 = (bf16[48,1728]{0,1:T(8,128)(2,1)S(1)}, bf16[48,1728]{0,1:T(8,128)(2,1)S(1)}, u32[]{:S(2)}, u32[]{:S(2)}) collective-permute-start(bf16[48,1728]{0,1:T(8,128)(2,1)S(1)} %slice.39), channel_id=1, source_target_pairs={{0,12},{1,13},{2,14},{3,15},{4,0},{5,1},{6,2},{7,3},{8,4},{9,5},{1... | collective-permute-start | bytes 497672 | tf_op jit(solution)/shard_map/ppermute | solution.py:36
  58.0 4.4 %collective-permute-start.8 = (bf16[128,1728]{0,1:T(8,128)(2,1)S(1)}, bf16[128,1728]{0,1:T(8,128)(2,1)}, u32[]{:S(2)}, u32[]{:S(2)}) collective-permute-start(bf16[128,1728]{0,1:T(8,128)(2,1)S(1)} %pad_maximum_fusion.4), channel_id=1, source_target_pairs={{0,1},{1,0},{2,3},{3,2},{4,5},{5,4},{6,7},{7,6},{8,9},{9,8},{10,11... | collective-permute-start | bytes 1327112 | tf_op jit(solution)/shard_map/ppermute | solution.py:36
  72.9 11.7 %collective-permute-start.13 = (bf16[128,1152]{1,0:T(8,128)(2,1)S(1)}, bf16[128,1152]{1,0:T(8,128)(2,1)S(1)}, u32[]{:S(2)}, u32[]{:S(2)}) collective-permute-start(bf16[128,1152]{1,0:T(8,128)(2,1)S(1)} %get-tuple-element.11), channel_id=1, source_target_pairs={{0,112},{16,0},{32,16},{48,32},{64,48},{80,64},{96,80},{112,96},{1... | collective-permute-start | bytes 884744 | tf_op jit(solution)/shard_map/ppermute | solution.py:17
  77.7 11.5 %collective-permute-start.17 = (bf16[128,1152]{1,0:T(8,128)(2,1)S(1)}, bf16[128,1152]{1,0:T(8,128)(2,1)S(1)}, u32[]{:S(2)}, u32[]{:S(2)}) collective-permute-start(bf16[128,1152]{1,0:T(8,128)(2,1)S(1)} %get-tuple-element.12), channel_id=1, source_target_pairs={{0,16},{16,32},{32,48},{48,64},{64,80},{80,96},{96,112},{112,0},{1... | collective-permute-start | bytes 884744 | tf_op jit(solution)/shard_map/ppermute | solution.py:17
  85.5 16.5 %collective-permute-start.14 = (bf16[256,1152]{1,0:T(8,128)(2,1)}, bf16[256,1152]{1,0:T(8,128)(2,1)}, u32[]{:S(2)}, u32[]{:S(2)}) collective-permute-start(bf16[256,1152]{1,0:T(8,128)(2,1)} %pad_maximum_fusion.2), channel_id=1, source_target_pairs={{0,112},{16,0},{32,16},{48,32},{64,48},{80,64},{96,80},{112,96},{1... | collective-permute-start | bytes 1769480 | tf_op jit(solution)/shard_map/ppermute | solution.py:17
  90.1 20.3 %collective-permute-start.18 = (bf16[256,1152]{1,0:T(8,128)(2,1)}, bf16[256,1152]{1,0:T(8,128)(2,1)}, u32[]{:S(2)}, u32[]{:S(2)}) collective-permute-start(bf16[256,1152]{1,0:T(8,128)(2,1)} %pad_maximum_fusion.3), channel_id=1, source_target_pairs={{0,16},{16,32},{32,48},{48,64},{64,80},{80,96},{96,112},{112,0},{1... | collective-permute-start | bytes 1769480 | tf_op jit(solution)/shard_map/ppermute | solution.py:17
  106.7 15.6 %collective-permute-start.15 = (bf16[256,1152]{1,0:T(8,128)(2,1)}, bf16[256,1152]{1,0:T(8,128)(2,1)}, u32[]{:S(2)}, u32[]{:S(2)}) collective-permute-start(bf16[256,1152]{1,0:T(8,128)(2,1)} %fusion.2), channel_id=1, source_target_pairs={{0,112},{16,0},{32,16},{48,32},{64,48},{80,64},{96,80},{112,96},{1... | collective-permute-start | bytes 1769480 | tf_op jit(solution)/shard_map/ppermute | solution.py:17
  114.0 16.8 %collective-permute-start.19 = (bf16[256,1152]{1,0:T(8,128)(2,1)}, bf16[256,1152]{1,0:T(8,128)(2,1)}, u32[]{:S(2)}, u32[]{:S(2)}) collective-permute-start(bf16[256,1152]{1,0:T(8,128)(2,1)} %fusion.4), channel_id=1, source_target_pairs={{0,16},{16,32},{32,48},{48,64},{64,80},{80,96},{96,112},{112,0},{1... | collective-permute-start | bytes 1769480 | tf_op jit(solution)/shard_map/ppermute | solution.py:17
  127.0 14.6 %collective-permute-start.16 = (bf16[256,1152]{1,0:T(8,128)(2,1)}, bf16[256,1152]{1,0:T(8,128)(2,1)}, u32[]{:S(2)}, u32[]{:S(2)}) collective-permute-start(bf16[256,1152]{1,0:T(8,128)(2,1)} %fusion.1), channel_id=1, source_target_pairs={{0,112},{16,0},{32,16},{48,32},{64,48},{80,64},{96,80},{112,96},{1... | collective-permute-start | bytes 1769480 | tf_op jit(solution)/shard_map/ppermute | solution.py:17
  134.3 14.4 %collective-permute-start.20 = (bf16[256,1152]{1,0:T(8,128)(2,1)}, bf16[256,1152]{1,0:T(8,128)(2,1)}, u32[]{:S(2)}, u32[]{:S(2)}) collective-permute-start(bf16[256,1152]{1,0:T(8,128)(2,1)} %fusion.3), channel_id=1, source_target_pairs={{0,16},{16,32},{32,48},{48,64},{64,80},{80,96},{96,112},{112,0},{1... | collective-permute-start | bytes 1769480 | tf_op jit(solution)/shard_map/ppermute | solution.py:17
  152.8 13.5 %collective-permute-start.21 = (bf16[256,1152]{1,0:T(8,128)(2,1)S(1)}, bf16[256,1152]{1,0:T(8,128)(2,1)S(1)}, u32[]{:S(2)}, u32[]{:S(2)}) collective-permute-start(bf16[256,1152]{1,0:T(8,128)(2,1)S(1)} %get-tuple-element.13), channel_id=1, source_target_pairs={{0,128},{16,144},{32,160},{48,176},{64,192},{80,208},{96,224},{112... | collective-permute-start | bytes 1769480 | tf_op jit(solution)/shard_map/ppermute | solution.py:22
  (9 other events, 87.7 us)
Sparse Core Ops, SparseCore 0:
  13.2 39.2 all-gather.5
  167.4 59.4 all-gather.3
